TPU v7x, 32 devices: a whole 2x2x4 slice. The times are simulated.
32 devices in a mesh: grp: 8 (over z, x), rep: 4 (over y, core).
Axes of the slice: x: 2, y: 2, z: 4, core: 2. Of those that a mesh axis runs over, the one named last changes fastest.
Arguments:
- series: bfloat16 [256, 5632], P('grp'), may hold values from -6 to 6
- regressors: float32 [256, 24], P('grp'), may hold values from -3 to 3
- span_ids: int32 [256], replicated, may hold values from 0 to 3, never falling along the last dimension, each value on 1 to 128 neighbouring positions
- nuisance_count: int32 [1], replicated, may hold values from 12 to 24
- owner_order: int32 [8], replicated, may hold values from 0 to 7
- vectors: bfloat16 [5632, 64], P('grp'), may hold values from -0.3125 to 0.3125
Outputs:
- projected: float32 [5632, 64], P(('grp', 'rep'))
Inputs may be any that keep to these rules, and one draw needn't show every extreme that they name: `span_ids`: never falls along frames; each of the 4 spans holds 1 to 128 frames, one exactly 128. `owner_order`: blocks may name the same slab.
All inputs are finite; a program needn't handle non-finite values.
Results may differ from a plain program's by a relative error of at most 0.0095.
Values may be sent and summed in bfloat16 or wider, within the bound.
A program may use at most 64 MiB of HBM per device.

v0:
```python
import math

import jax
import jax.numpy as jnp
from jax import lax
from jax.sharding import PartitionSpec as P

BLOCKS = 8


fast_pole = 0.64
slow_pole = 0.955
corr_limit = 0.99
norm_eps = 1e-06


def spread_2(value, axis, root):
    mine = lax.axis_index(axis) == root
    return lax.psum(jnp.where(mine, value, jnp.zeros_like(value)), axis)


def fisher_map(correlation):
    clipped = jnp.clip(correlation, -corr_limit, corr_limit)
    return 0.5 * jnp.log((1.0 + clipped) / (1.0 - clipped))


def block_operators(span_ids, frames):
    offsets = jnp.arange(128)
    lag_steps = offsets[:, None] - offsets[None, :]
    lag_clip = jnp.maximum(lag_steps, 0).astype(jnp.float32)
    operators = []
    for number in range(frames // 128):
        ids_here = span_ids[number * 128 : (number + 1) * 128]
        joined = (ids_here[:, None] == ids_here[None, :]) & (lag_steps >= 0)
        if number == 0:
            linked = jnp.zeros((128,), jnp.float32)
        else:
            linked = (ids_here == span_ids[number * 128 - 1]).astype(jnp.float32)
        pole_pair = []
        for pole_value in (fast_pole, slow_pole):
            matrix = jnp.where(
                joined, (1.0 - pole_value) * jnp.exp(lag_clip * math.log(pole_value)), 0.0
            )
            carried = linked * jnp.exp((offsets + 1).astype(jnp.float32) * math.log(pole_value))
            pole_pair.append((matrix, carried))
        operators.append(pole_pair)
    return operators


def band_pass(columns_in, operators):
    col_count = columns_in.shape[1]
    states = [jnp.zeros((col_count,), jnp.float32), jnp.zeros((col_count,), jnp.float32)]
    pieces = []
    for number, pole_pair in enumerate(operators):
        segment = columns_in[number * 128 : (number + 1) * 128]
        outputs = []
        for pole_slot in range(2):
            matrix, carried = pole_pair[pole_slot]
            response = (
                jnp.dot(matrix, segment, precision=lax.Precision.HIGHEST)
                + carried[:, None] * states[pole_slot][None, :]
            )
            states[pole_slot] = response[-1]
            outputs.append(response)
        pieces.append(outputs[0] - outputs[1])
    return jnp.concatenate(pieces, axis=0)


def nuisance_basis(filtered_nuisance, nuisance_count):
    active = (jnp.arange(filtered_nuisance.shape[1]) < nuisance_count[0]).astype(jnp.float32)
    masked = filtered_nuisance * active[None, :]
    gram_matrix = jnp.dot(masked.T, masked, precision=lax.Precision.HIGHEST) + jnp.diag(
        1.0 - active
    )
    return (masked, jnp.linalg.cholesky(gram_matrix))


def scale_columns(filtered, masked, lower_factor):
    highest = lax.Precision.HIGHEST
    right_side = jnp.dot(masked.T, filtered, precision=highest)
    halfway = lax.linalg.triangular_solve(lower_factor, right_side, left_side=True, lower=True)
    coefficients = lax.linalg.triangular_solve(
        lower_factor, halfway, left_side=True, lower=True, transpose_a=True
    )
    cleaned = filtered - jnp.dot(masked, coefficients, precision=highest)
    centered = cleaned - jnp.mean(cleaned, axis=0, keepdims=True)
    spread = lax.rsqrt(jnp.mean(centered * centered, axis=0, keepdims=True) + norm_eps)
    return (centered * spread * (1.0 / math.sqrt(centered.shape[0]))).astype(jnp.bfloat16)


def fold_tile(my_cols, vec_slab, running, part_cols):
    correlation = lax.dot_general(
        my_cols, part_cols, (((0,), (0,)), ((), ())), preferred_element_type=jnp.float32
    )
    fisher = fisher_map(correlation).astype(jnp.bfloat16)
    return running + jnp.dot(fisher, vec_slab, preferred_element_type=jnp.float32)


def local(series, regressors, span_ids, nuisance_count, owner_order, vectors):
    grp_count = lax.axis_size("grp")
    rep_count = lax.axis_size("rep")
    rep_index = lax.axis_index("rep")
    frames_loc = series.shape[0]
    frames = frames_loc * grp_count
    own_cols = series.shape[1] // (grp_count * rep_count)
    operators = block_operators(span_ids, frames)
    nuisance = lax.all_gather(regressors, "grp", axis=0, tiled=True)
    masked, lower_factor = nuisance_basis(band_pass(nuisance, operators), nuisance_count)
    quarter = series.reshape(frames_loc, grp_count, rep_count, own_cols)
    quarter = lax.dynamic_slice_in_dim(quarter, rep_index, 1, 2).reshape(
        frames_loc, grp_count, own_cols
    )
    filtered = band_pass(
        lax.all_to_all(quarter, "grp", split_axis=1, concat_axis=0, tiled=True)[:, 0, :].astype(
            jnp.float32
        ),
        operators,
    )
    unit_cols = scale_columns(filtered, masked, lower_factor)
    projected = jnp.zeros((own_cols, vectors.shape[1]), jnp.float32)
    for number in range(BLOCKS):
        piece_in, vec_slab = (
            spread_2(unit_cols, "grp", owner_order[number]),
            spread_2(vectors, "grp", owner_order[number]),
        )
        projected = fold_tile(
            unit_cols, vec_slab, projected, lax.all_gather(piece_in, "rep", axis=1, tiled=True)
        )
    return projected


def solution(mesh):
    placed = (P("grp", None), P("grp", None), P(), P(), P(), P("grp", None))
    return jax.shard_map(
        local, mesh=mesh, in_specs=placed, out_specs=P(("grp", "rep"), None), check_vma=False
    )
```

profile of v0, /device:TPU:0, one launch (start us, length us, event | category | flops | bytes accessed | tf_op | source)
XLA Modules:
  0.0 231.1 jit_solution(4362847719951692597)
XLA Ops:
  6.5 2.0 reshape.62
  8.5 0.3 constant_dynamic-slice_fusion
  8.8 0.7 copy.24
  9.6 7.3 %all-to-all-start = ((bf16[32,8,176]{2,0,1:T(8,128)(2,1)}), bf16[32,8,176]{2,0,1:T(8,128)(2,1)S(1)}, u32[]{:S(2)}, u32[]{:S(2)}) async-start(bf16[32,8,176]{2,0,1:T(8,128)(2,1)} %bitcast.70), calls=%async_computation | async-start | bytes 262144 | tf_op jit(solution)/shard_map/all_to_all | solution.py:114
  16.9 0.7 copy-done.10
  17.5 0.6 slice.91
  18.8 0.7 compare_select_fusion
  19.5 0.7 fusion.173
  25.2 31.1 %all-gather = f32[8,32,24]{1,2,0:T(8,128)S(1)} all-gather(f32[1,32,24]{1,2,0:T(8,128)S(1)} %bitcast.78), channel_id=1, replica_groups=mesh['grp'=8,'rep'=4] {'grp'}, dimensions={0}, use_global_device_ids=true | all-gather | bytes 27648 | tf_op jit(solution)/shard_map/all_gather | solution.py:107
  56.9 0.3 fusion.175
  57.7 0.3 fusion.1
  58.4 2.2 cholesky.16
  60.7 0.6 compare_reduce_fusion
  61.3 0.6 fusion.93
  62.0 1.9 custom-call.8
  63.8 0.9 broadcast_select_fusion
  64.8 0.3 convolution_add_fusion.2
  65.2 0.3 fusion.174
  65.7 0.3 convolution_add_fusion.1
  66.0 0.3 fusion
  66.3 0.3 fusion.35
  67.0 0.5 fusion.176
  67.6 0.8 broadcast_select_fusion.8
  68.4 0.9 broadcast_select_fusion.9
  69.3 95.1 %all-reduce.3.cloned.1.call-done = (bf16[704,64]{0,1:T(8,128)(2,1)}, bf16[256,176]{0,1:T(8,128)(2,1)}, bf16[704,64]{0,1:T(8,128)(2,1)}, bf16[256,176]{0,1:T(8,12...) async-done(((bf16[704,64]{0,1:T(8,128)(2,1)}, ...) | async-done | bytes 1441808 | tf_op jit(solution)/shard_map/psum | solution.py:19
  164.5 6.7 %all_gather.28 = bf16[256,704]{0,1:T(8,128)(2,1)S(1)} all-gather(bf16[256,176]{0,1:T(8,128)(2,1)} %get-tuple-element.6), channel_id=1, replica_groups=mesh['grp'=8,'rep'=4] {'rep'}, dimensions={1}, use_global_device_ids=true | all-gather | bytes 450560 | tf_op jit(solution)/shard_map/all_gather | solution.py:127
  171.2 6.5 %all_gather.29 = bf16[256,704]{0,1:T(8,128)(2,1)S(1)} all-gather(bf16[256,176]{0,1:T(8,128)(2,1)S(1)} %copy-done.7), channel_id=1, replica_groups=mesh['grp'=8,'rep'=4] {'rep'}, dimensions={1}, use_global_device_ids=true | all-gather | bytes 450560 | tf_op jit(solution)/shard_map/all_gather | solution.py:127
  177.7 6.5 %all_gather.30 = bf16[256,704]{0,1:T(8,128)(2,1)S(1)} all-gather(bf16[256,176]{0,1:T(8,128)(2,1)S(1)} %copy-done.6), channel_id=1, replica_groups=mesh['grp'=8,'rep'=4] {'rep'}, dimensions={1}, use_global_device_ids=true | all-gather | bytes 450560 | tf_op jit(solution)/shard_map/all_gather | solution.py:127
  184.2 6.5 %all_gather.31 = bf16[256,704]{0,1:T(8,128)(2,1)S(1)} all-gather(bf16[256,176]{0,1:T(8,128)(2,1)S(1)} %copy-done.5), channel_id=1, replica_groups=mesh['grp'=8,'rep'=4] {'rep'}, dimensions={1}, use_global_device_ids=true | all-gather | bytes 450560 | tf_op jit(solution)/shard_map/all_gather | solution.py:127
  190.7 6.5 %all_gather.32 = bf16[256,704]{0,1:T(8,128)(2,1)S(1)} all-gather(bf16[256,176]{0,1:T(8,128)(2,1)S(1)} %copy-done.4), channel_id=1, replica_groups=mesh['grp'=8,'rep'=4] {'rep'}, dimensions={1}, use_global_device_ids=true | all-gather | bytes 450560 | tf_op jit(solution)/shard_map/all_gather | solution.py:127
  197.3 6.5 %all_gather.33 = bf16[256,704]{0,1:T(8,128)(2,1)S(1)} all-gather(bf16[256,176]{0,1:T(8,128)(2,1)S(1)} %copy-done.3), channel_id=1, replica_groups=mesh['grp'=8,'rep'=4] {'rep'}, dimensions={1}, use_global_device_ids=true | all-gather | bytes 450560 | tf_op jit(solution)/shard_map/all_gather | solution.py:127
  203.8 6.5 %all_gather.34 = bf16[256,704]{0,1:T(8,128)(2,1)S(1)} all-gather(bf16[256,176]{0,1:T(8,128)(2,1)S(1)} %copy-done.2), channel_id=1, replica_groups=mesh['grp'=8,'rep'=4] {'rep'}, dimensions={1}, use_global_device_ids=true | all-gather | bytes 450560 | tf_op jit(solution)/shard_map/all_gather | solution.py:127
  210.3 6.5 %all_gather.35 = bf16[256,704]{0,1:T(8,128)(2,1)S(1)} all-gather(bf16[256,176]{0,1:T(8,128)(2,1)S(1)} %copy-done.1), channel_id=1, replica_groups=mesh['grp'=8,'rep'=4] {'rep'}, dimensions={1}, use_global_device_ids=true | all-gather | bytes 450560 | tf_op jit(solution)/shard_map/all_gather | solution.py:127
  216.8 0.5 fusion.2
  217.3 0.4 copy-done.17
  217.7 0.5 convolution_add_fusion.10
  218.2 0.4 copy-done.16
  218.6 0.5 convolution_add_fusion.9
  219.1 0.4 copy-done.15
  219.5 0.5 convolution_add_fusion.8
  220.0 0.4 copy-done.14
  220.4 0.5 convolution_add_fusion.7
  220.9 0.4 copy-done.13
  221.3 0.5 convolution_add_fusion.6
  221.8 0.4 copy-done.12
  222.2 0.5 convolution_add_fusion.5
  222.7 0.4 copy-done.11
  223.1 1.1 convolution_add_fusion.4
  (59 shorter events, 2.6 us)
Async XLA Ops:
  9.6 55.2 %all-to-all-start = ((bf16[32,8,176]{2,0,1:T(8,128)(2,1)}), bf16[32,8,176]{2,0,1:T(8,128)(2,1)S(1)}, u32[]{:S(2)}, u32[]{:S(2)}) async-start(bf16[32,8,176]{2,0,1:T(8,128)(2,1)} %bitcast.70), calls=%async_computation | async-start | bytes 262144 | tf_op jit(solution)/shard_map/all_to_all | solution.py:114
  16.8 147.6 %all-reduce.3.cloned.1.call-start = ((), (), s32[]{:S(2)}) async-start(), calls=%async_computation.1 | async-start | bytes 3014656 | tf_op jit(solution)/shard_map/psum | solution.py:19
  16.9 0.7 copy-start.10
  18.8 0.7 copy-start.8
  22.6 2.6 %copy-start.9 = (f32[32,24]{0,1:T(8,128)S(1)}, f32[32,24]{0,1:T(8,128)}, u32[]{:S(2)}) copy-start(f32[32,24]{0,1:T(8,128)} %param.7) | copy-start | bytes 9220
  58.1 5.8 %copy-start = (bf16[704,64]{0,1:T(8,128)(2,1)S(1)}, bf16[704,64]{0,1:T(8,128)(2,1)}, u32[]{:S(2)}) copy-start(bf16[704,64]{0,1:T(8,128)(2,1)} %param.11) | copy-start | bytes 270340
  164.5 6.7 %copy-start.7 = (bf16[256,176]{0,1:T(8,128)(2,1)S(1)}, bf16[256,176]{0,1:T(8,128)(2,1)}, u32[]{:S(2)}) copy-start(bf16[256,176]{0,1:T(8,128)(2,1)} %get-tuple-element.8) | copy-start | bytes 270340
  171.2 6.5 %copy-start.6 = (bf16[256,176]{0,1:T(8,128)(2,1)S(1)}, bf16[256,176]{0,1:T(8,128)(2,1)}, u32[]{:S(2)}) copy-start(bf16[256,176]{0,1:T(8,128)(2,1)} %get-tuple-element.10) | copy-start | bytes 270340
  177.7 6.5 %copy-start.5 = (bf16[256,176]{0,1:T(8,128)(2,1)S(1)}, bf16[256,176]{0,1:T(8,128)(2,1)}, u32[]{:S(2)}) copy-start(bf16[256,176]{0,1:T(8,128)(2,1)} %get-tuple-element.12) | copy-start | bytes 270340
  184.2 6.5 %copy-start.4 = (bf16[256,176]{0,1:T(8,128)(2,1)S(1)}, bf16[256,176]{0,1:T(8,128)(2,1)}, u32[]{:S(2)}) copy-start(bf16[256,176]{0,1:T(8,128)(2,1)} %get-tuple-element.14) | copy-start | bytes 270340
  190.7 6.5 %copy-start.3 = (bf16[256,176]{0,1:T(8,128)(2,1)S(1)}, bf16[256,176]{0,1:T(8,128)(2,1)}, u32[]{:S(2)}) copy-start(bf16[256,176]{0,1:T(8,128)(2,1)} %get-tuple-element.16) | copy-start | bytes 270340
  197.3 6.5 %copy-start.2 = (bf16[256,176]{0,1:T(8,128)(2,1)S(1)}, bf16[256,176]{0,1:T(8,128)(2,1)}, u32[]{:S(2)}) copy-start(bf16[256,176]{0,1:T(8,128)(2,1)} %get-tuple-element.18) | copy-start | bytes 270340
  203.8 6.5 %copy-start.1 = (bf16[256,176]{0,1:T(8,128)(2,1)S(1)}, bf16[256,176]{0,1:T(8,128)(2,1)}, u32[]{:S(2)}) copy-start(bf16[256,176]{0,1:T(8,128)(2,1)} %get-tuple-element.20) | copy-start | bytes 270340
  210.3 6.5 %copy-start.18 = (bf16[704,64]{0,1:T(8,128)(2,1)S(1)}, bf16[704,64]{0,1:T(8,128)(2,1)}, u32[]{:S(2)}) copy-start(bf16[704,64]{0,1:T(8,128)(2,1)} %get-tuple-element.5) | copy-start | bytes 270340
  216.8 0.9 copy-start.17
  217.7 0.9 copy-start.16
  218.6 0.9 copy-start.15
  219.5 0.9 copy-start.14
  220.4 0.9 copy-start.13
  221.3 0.9 copy-start.12
  222.2 0.9 copy-start.11
Sparse Core Ops, SparseCore 0:
  69.4 94.9 all-reduce.2
where the time goes:
time: 232 us; the launch traced here: 231 us
  waiting for transfers between devices  95.1 us (41%)
  blocking collectives  83.4 us (36%)
  between operations  19.4 us (8%)
  other arithmetic  8.9 us (4%)
  local copies, waits for them, and re-layouts  8.67 us (4%)
  matrix products  8.23 us (4%)
  starting transfers between devices  7.29 us (3%)
    psum x1, waiting for transfers between devices, spread_2(): return lax.psum(jnp.where(mine, value, jnp.zeros_like(value)), axis)  95.1 us
    all_gather x8, blocking collectives, local(): lax.all_gather(piece_in, 'rep', axis=1, tiled=True)  52.3 us
    all_gather x1, blocking collectives, local(): nuisance = lax.all_gather(regressors, 'grp', axis=0, tiled=True)  31.1 us
    all_to_all x1, starting transfers between devices, local(): lax.all_to_all(quarter, 'grp', split_axis=1, concat_axis=0, tiled=True)  7.25 us
    dot_general x8, matrix products, fold_tile(): jnp.dot(fisher, vec_slab, preferred_element_type=jnp.float32)  4.66 us
  transfers between devices with their start and end apart: 2, of which 1 were waited for; matrix products, arithmetic and copies ran while one was open for 4% of the time, Pallas kernels for 0%

commit v1 on v0

--- a/solution.py
+++ b/solution.py
@@ -1,17 +1,351 @@
+import functools
 import math
 
 import jax
 import jax.numpy as jnp
 from jax import lax
+from jax.experimental import pallas as pl
+from jax.experimental.pallas import tpu as pltpu
 from jax.sharding import PartitionSpec as P
 
 BLOCKS = 8
-
+MESH = pl.DeviceIdType.MESH
+HIGHEST = lax.Precision.HIGHEST
 
 fast_pole = 0.64
 slow_pole = 0.955
 corr_limit = 0.99
 norm_eps = 1e-06
+
+
+def dot32(a, b, ca, cb):
+    return lax.dot_general(
+        a, b, (((ca,), (cb,)), ((), ())), precision=HIGHEST, preferred_element_type=jnp.float32
+    )
+
+
+def dot16(a, b, ca, cb):
+    return lax.dot_general(
+        a, b, (((ca,), (cb,)), ((), ())), preferred_element_type=jnp.float32
+    )
+
+
+def band_matrix(span_row):
+    frames = span_row.shape[1]
+    across = jnp.broadcast_to(span_row.astype(jnp.float32), (frames, frames))
+    down = across.T
+    lag = lax.broadcasted_iota(jnp.int32, (frames, frames), 0) - lax.broadcasted_iota(
+        jnp.int32, (frames, frames), 1
+    )
+    steps = jnp.maximum(lag, 0).astype(jnp.float32)
+    fast = (1.0 - fast_pole) * jnp.exp(steps * math.log(fast_pole))
+    slow = (1.0 - slow_pole) * jnp.exp(steps * math.log(slow_pole))
+    return jnp.where((lag >= 0) & (across == down), fast - slow, 0.0)
+
+
+def spd_inverse(gram):
+    size = gram.shape[0]
+    lane = lax.broadcasted_iota(jnp.int32, (size, size), 1)
+    sub = lax.broadcasted_iota(jnp.int32, (size, size), 0)
+
+    def sweep(k, m):
+        on_col, on_row = lane == k, sub == k
+        col = jnp.sum(jnp.where(on_col, m, 0.0), axis=1, keepdims=True)
+        row = jnp.sum(jnp.where(on_row, m, 0.0), axis=0, keepdims=True)
+        pivot = jnp.sum(jnp.where(on_col & on_row, m, 0.0), axis=(0, 1), keepdims=True)
+        inv = 1.0 / pivot
+        rest = m - col * (row * inv)
+        return jnp.where(
+            on_row,
+            jnp.where(on_col, inv, row * inv),
+            jnp.where(on_col, -col * inv, rest),
+        )
+
+    return lax.fori_loop(0, size, sweep, gram)
+
+
+def kernel(
+    series, regs, span, count, owner, vectors, out,
+    win, rows, nreg, vto, vtb, vtf, a_hi, a_lo, unit_rows, parts, other,
+    send, reg_r, win_r, core_r, vt_r, vtc_r, rows_r, fin_r, loc,
+):
+    grp, rep = lax.axis_index("grp"), lax.axis_index("rep")
+    z, x = grp // 2, grp % 2
+    y, c = rep // 2, rep % 2
+    groups = lax.axis_size("grp")
+    nz = groups // 2
+    frames_loc, gray = series.shape
+    half = gray // 2
+    piece = half // 2
+    slab = gray // groups
+    wide = rows.shape[1]
+    per_half = groups // 2
+    quarter = out.shape[0]
+    home = z // (nz // 2) == y
+    away = z // (nz // 2) != y
+    mine = grp % per_half
+
+    def at(zz, xx, yy, cc):
+        return (zz * 2 + xx, yy * 2 + cc)
+
+    zs = [lax.rem(z + d, nz) for d in range(1, nz)]
+    x_peer = at(z, 1 - x, y, c)
+    core_peer = at(z, x, y, 1 - c)
+    y_peer = at(z, x, 1 - y, c)
+
+    barrier = pltpu.get_barrier_semaphore()
+    everyone = [at(zz, x, y, c) for zz in zs] + [x_peer, core_peer, y_peer]
+    for peer in everyone:
+        pl.semaphore_signal(barrier, inc=1, device_id=peer, device_id_type=MESH)
+
+    sent = []
+    counter = [0]
+
+    def push(src, dst, recv, peer, cond=None):
+        k = counter[0]
+        counter[0] += 1
+        copy = pltpu.make_async_remote_copy(
+            src_ref=src, dst_ref=dst, send_sem=send.at[k], recv_sem=recv,
+            device_id=peer, device_id_type=MESH,
+        )
+        if cond is None:
+            copy.start()
+        else:
+            pl.when(cond)(copy.start)
+        sent.append((copy, cond))
+
+    def arrive(dst, recv):
+        pltpu.make_async_copy(dst, dst, recv).wait()
+
+    def rows_of(s):
+        return pl.ds(pl.multiple_of(s * frames_loc, frames_loc), frames_loc)
+
+    own_cols = pl.ds(pl.multiple_of(c * piece, 128), piece)
+    core_cols = pl.ds(pl.multiple_of((1 - c) * piece, 128), piece)
+    series_cols = pl.ds(pl.multiple_of(y * half + c * piece, 128), piece)
+    slab_at = pl.multiple_of(grp * slab - (slab % 128) * x, 128)
+    slab_in_half = pl.multiple_of(mine * slab - (slab % 128) * x, 128)
+    vt_half = pl.ds(pl.multiple_of(c * 32, 32), 32)
+    vt_other = pl.ds(pl.multiple_of((1 - c) * 32, 32), 32)
+
+    local_win = pltpu.make_async_copy(
+        series.at[:, pl.ds(pl.multiple_of(y * half, 128), half)], win.at[rows_of(grp), :], loc.at[0]
+    )
+    local_rows = pltpu.make_async_copy(
+        series.at[:, pl.ds(slab_at, wide)], rows.at[rows_of(grp), :], loc.at[1]
+    )
+    local_win.start()
+    local_rows.start()
+    nreg[rows_of(grp), :] = regs[...]
+    nvec = vectors.shape[1]
+    eye = (
+        lax.broadcasted_iota(jnp.int32, (nvec, nvec), 0)
+        == lax.broadcasted_iota(jnp.int32, (nvec, nvec), 1)
+    ).astype(jnp.float32).astype(jnp.bfloat16)
+    vto[...] = dot16(eye, vectors[...], 1, 1).astype(jnp.bfloat16)
+
+    @pl.when(home)
+    def _():
+        vtb[mine] = vto[...]
+
+    pl.semaphore_wait(barrier, len(everyone))
+
+    for zz in zs + [None]:
+        peer = x_peer if zz is None else at(zz, x, y, c)
+        push(regs, nreg.at[rows_of(grp), :], reg_r.at[grp], peer)
+    for zz in zs + [None]:
+        peer = x_peer if zz is None else at(zz, x, y, c)
+        push(series.at[:, series_cols], win.at[rows_of(grp), own_cols], win_r.at[grp], peer)
+    for zz in zs + [None]:
+        peer = x_peer if zz is None else at(zz, x, y, c)
+        push(vto.at[vt_half, :], vtb.at[mine, vt_half, :], vt_r.at[mine], peer, home)
+
+    filt = band_matrix(span[...])
+
+    back = [lax.rem(z + nz - d, nz) for d in range(1, nz)]
+    for zz in back:
+        s = zz * 2 + x
+        arrive(nreg.at[rows_of(s), :], reg_r.at[s])
+        push(nreg.at[rows_of(s), :], nreg.at[rows_of(s), :], reg_r.at[s], x_peer)
+
+    def from_z(zz):
+        s = zz * 2 + x
+        here = win.at[rows_of(s), own_cols]
+        arrive(here, win_r.at[s])
+        push(here, here, win_r.at[s], x_peer)
+        push(here, here, core_r.at[s], core_peer)
+
+    from_z(back[0])
+
+    for zz in [z] + back:
+        s = zz * 2 + 1 - x
+        arrive(nreg.at[rows_of(s), :], reg_r.at[s])
+
+    kmax = regs.shape[1]
+    active = (lax.broadcasted_iota(jnp.int32, (1, kmax), 1) < count[0]).astype(jnp.float32)
+    masked = dot32(filt, nreg[...], 1, 0) * active
+    diag = (
+        lax.broadcasted_iota(jnp.int32, (kmax, kmax), 0)
+        == lax.broadcasted_iota(jnp.int32, (kmax, kmax), 1)
+    )
+    gram = dot32(masked, masked, 0, 0) + jnp.where(diag, 1.0 - active, 0.0)
+    inverse = spd_inverse(gram)
+
+    for zz in back[1:]:
+        from_z(zz)
+
+    for zz in back:
+        s = zz * 2 + x
+        t = lax.rem(s, per_half)
+        want = zz // (nz // 2) == y
+        here = vtb.at[t, vt_half, :]
+
+        def took(here=here, t=t):
+            arrive(here, vt_r.at[t])
+
+        pl.when(want)(took)
+        push(here, here, vt_r.at[t], x_peer, want)
+        push(here, here, vtc_r.at[t], core_peer, want)
+
+    fitted = dot32(inverse, dot32(masked, filt, 0, 0), 1, 0)
+    clean = filt - dot32(masked, fitted, 1, 0)
+    clean = clean - jnp.mean(clean, axis=0, keepdims=True)
+    hi = clean.astype(jnp.bfloat16)
+    a_hi[...] = hi
+    a_lo[...] = (clean - hi.astype(jnp.float32)).astype(jnp.bfloat16)
+
+    for zz in [z] + back:
+        s = zz * 2 + 1 - x
+        here = win.at[rows_of(s), own_cols]
+        arrive(here, win_r.at[s])
+        push(here, here, core_r.at[s], core_peer)
+
+    for zz in [z] + back:
+        s = zz * 2 + 1 - x
+        t = lax.rem(s, per_half)
+        want = zz // (nz // 2) == y
+        here = vtb.at[t, vt_half, :]
+
+        def took(here=here, t=t):
+            arrive(here, vt_r.at[t])
+
+        pl.when(want)(took)
+        push(here, here, vtc_r.at[t], core_peer, want)
+
+    order = [zz * 2 + x for zz in back] + [zz * 2 + 1 - x for zz in [z] + back]
+    inner = []
+    for n, s in enumerate(order):
+        arrive(win.at[rows_of(s), core_cols], core_r.at[s])
+        src = win.at[rows_of(s), pl.ds(slab_in_half, wide)]
+        push(src, rows.at[rows_of(s), :], rows_r.at[s], y_peer, home)
+        keep = pltpu.make_async_copy(src, rows.at[rows_of(s), :], loc.at[2 + n])
+        pl.when(home)(keep.start)
+        inner.append(keep)
+
+    local_win.wait()
+    local_rows.wait()
+
+    for xx, list_z in ((x, back), (1 - x, [z] + back)):
+        for zz in list_z:
+            t = lax.rem(zz * 2 + xx, per_half)
+            want = zz // (nz // 2) == y
+
+            def took(t=t):
+                arrive(vtb.at[t, vt_other, :], vtc_r.at[t])
+
+            pl.when(want)(took)
+    vtf[...] = jnp.concatenate([vtb[t] for t in range(per_half)], axis=1)
+
+    def normal(block):
+        centered = dot16(a_hi[...], block, 1, 0) + dot16(a_lo[...], block, 1, 0)
+        power = jnp.mean(centered * centered, axis=0, keepdims=True) + norm_eps
+        return centered * (lax.rsqrt(power) * (1.0 / math.sqrt(centered.shape[0])))
+
+    for n, s in enumerate(order):
+        def wait_away(s=s):
+            arrive(rows.at[rows_of(s), :], rows_r.at[s])
+
+        pl.when(away)(wait_away)
+        pl.when(home)(inner[n].wait)
+    unit_rows[...] = normal(rows[...]).T.astype(jnp.bfloat16)
+    first = (slab % 128) * x + quarter * c
+    left = jnp.concatenate(
+        [
+            unit_rows[pl.ds(pl.multiple_of(first + 2 * quarter * k, 16), quarter), :]
+            for k in range(2)
+        ],
+        axis=0,
+    )
+
+    width = 256
+    lane = lax.broadcasted_iota(jnp.int32, (1, width), 1)
+
+    def fold(j, total):
+        cols = pl.ds(pl.multiple_of(j * width, width), width)
+        unit = normal(win[:, cols]).astype(jnp.bfloat16)
+        corr = jnp.clip(dot16(left, unit, 1, 0), -corr_limit, corr_limit)
+        place = lane + j * width
+        which = jnp.full((1, width), y * per_half, jnp.int32)
+        for t in range(1, per_half):
+            which = which + (place >= t * slab).astype(jnp.int32)
+        times = jnp.zeros((1, width), jnp.float32)
+        for b in range(BLOCKS):
+            times = times + jnp.where(which == owner[b], 0.5, 0.0)
+        fisher = ((jnp.log(1.0 + corr) - jnp.log(1.0 - corr)) * times).astype(jnp.bfloat16)
+        return total + dot16(fisher, vtf[:, cols], 1, 1)
+
+    total = lax.fori_loop(
+        0, half // width, fold, jnp.zeros((2 * quarter, nvec), jnp.float32)
+    )
+    parts[0] = total[:quarter]
+    parts[1] = total[quarter:]
+    push(parts.at[1 - y], other, fin_r, y_peer)
+    arrive(other, fin_r)
+    out[...] = parts[y] + other[...]
+    for copy, cond in sent:
+        if cond is None:
+            copy.wait_send()
+        else:
+            pl.when(cond)(copy.wait_send)
+
+
+def one_kernel(series, regressors, span_ids, nuisance_count, owner_order, vectors):
+    groups, reps = lax.axis_size("grp"), lax.axis_size("rep")
+    frames_loc, gray = series.shape
+    frames = frames_loc * groups
+    slab = gray // groups
+    quarter = slab // reps
+    wide = -(-slab // 128) * 128
+    nvec = vectors.shape[1]
+    vm = pl.BlockSpec(memory_space=pltpu.VMEM)
+    sm = pl.BlockSpec(memory_space=pltpu.SMEM)
+    dma = pltpu.SemaphoreType.DMA
+    return pl.pallas_call(
+        kernel,
+        out_shape=jax.ShapeDtypeStruct((quarter, nvec), jnp.float32),
+        in_specs=[pl.BlockSpec(memory_space=pl.ANY), vm, vm, sm, sm, vm],
+        out_specs=vm,
+        scratch_shapes=[
+            pltpu.VMEM((frames, gray // 2), jnp.bfloat16),
+            pltpu.VMEM((frames, wide), jnp.bfloat16),
+            pltpu.VMEM((frames, regressors.shape[1]), jnp.float32),
+            pltpu.VMEM((nvec, slab), jnp.bfloat16),
+            pltpu.VMEM((groups // 2, nvec, slab), jnp.bfloat16),
+            pltpu.VMEM((nvec, gray // 2), jnp.bfloat16),
+            pltpu.VMEM((frames, frames), jnp.bfloat16),
+            pltpu.VMEM((frames, frames), jnp.bfloat16),
+            pltpu.VMEM((wide, frames), jnp.bfloat16),
+            pltpu.VMEM((2, quarter, nvec), jnp.float32),
+            pltpu.VMEM((quarter, nvec), jnp.float32),
+            dma((64,)),
+            dma((groups,)), dma((groups,)), dma((groups,)),
+            dma((groups // 2,)), dma((groups // 2,)),
+            dma((groups,)), dma, dma((16,)),
+        ],
+        compiler_params=pltpu.CompilerParams(
+            collective_id=0, has_side_effects=True, vmem_limit_bytes=40 * 1024 * 1024
+        ),
+    )(series, regressors, span_ids[None, :], nuisance_count, owner_order, vectors)
 
 
 def spread_2(value, axis, root):
@@ -96,7 +430,7 @@
     return running + jnp.dot(fisher, vec_slab, preferred_element_type=jnp.float32)
 
 
-def local(series, regressors, span_ids, nuisance_count, owner_order, vectors):
+def by_block(series, regressors, span_ids, nuisance_count, owner_order, vectors):
     grp_count = lax.axis_size("grp")
     rep_count = lax.axis_size("rep")
     rep_index = lax.axis_index("rep")
@@ -130,6 +464,7 @@
 
 
 def solution(mesh):
+    local = one_kernel if mesh.shape["grp"] <= BLOCKS else by_block
     placed = (P("grp", None), P("grp", None), P(), P(), P(), P("grp", None))
     return jax.shard_map(
         local, mesh=mesh, in_specs=placed, out_specs=P(("grp", "rep"), None), check_vma=False

time: 232 us -> 48 us (0.21)
  waiting for transfers between devices: 95.1 us -> 0 us
  blocking collectives: 83.4 us -> 0 us
  Pallas kernels: 0 us -> 43.5 us
  between operations: 19.4 us -> 0.68 us
  other arithmetic: 8.9 us -> 0 us
  matrix products: 8.23 us -> 0 us
  starting transfers between devices: 7.29 us -> 0 us
  local copies, waits for them, and re-layouts: 8.67 us -> 3.56 us
    psum x1 -> x0, waiting for transfers between devices: 95.1 us -> none  [spread_2(): return lax.psum(jnp.where(mine, value, jnp.zeros_like(value)), axis)]
    all_gather x9 -> x0, blocking collectives: 83.4 us -> none  [the longest x8 52.3 us: local(): lax.all_gather(piece_in, 'rep', axis=1, tiled=True)]
    pallas_call x0 -> x1, Pallas kernels: none -> 43.5 us  [one_kernel(): pl.pallas_call(kernel, out_shape=jax.ShapeDtypeStruct((quarter, nvec), jn...]
    dot_general x19 -> x0, matrix products: 7.88 us -> none  [the longest x8 4.66 us: fold_tile(): jnp.dot(fisher, vec_slab, preferred_element_type=jnp.float32)]
    all_to_all x1 -> x0, starting transfers between devices: 7.25 us -> none  [local(): lax.all_to_all(quarter, 'grp', split_axis=1, concat_axis=0, tiled=True)]
    another operation x5 -> x0, other arithmetic: 5.37 us -> none  [the longest x3 2.87 us: nuisance_basis(): return (masked, jnp.linalg.cholesky(gram_matrix))]
    reshape x2 -> x0, local copies, waits for them, and re-layouts: 2.72 us -> none  [the longest x1 1.98 us: local(): quarter = series.reshape(frames_loc, grp_count, rep_count, own_cols)]
    select_n x3 -> x0, other arithmetic: 2.56 us -> none  [spread_2(): return lax.psum(jnp.where(mine, value, jnp.zeros_like(value)), axis)]
  transfers between devices with their start and end apart: 2 -> 0, of which waited for: 1 -> 0; matrix products, arithmetic and copies ran while one was open for 4% -> 0% of each run, Pallas kernels for 0% -> 0%
where the time goes in v1:
time: 48 us; the launch traced here: 47.7 us
  Pallas kernels  43.5 us (91%)
  local copies, waits for them, and re-layouts  3.56 us (7%)
  between operations  0.68 us (1%)
    pallas_call x1, Pallas kernels, one_kernel(): pl.pallas_call(kernel, out_shape=jax.ShapeDtypeStruct((quarter, nvec), jn...  43.5 us
    unnamed x8, local copies, waits for them, and re-layouts  2.85 us

profile of v1, /device:TPU:0, one launch (start us, length us, event | category | flops | bytes accessed | tf_op | source)
XLA Modules:
  0.0 47.7 jit_solution(10214895669038910241)
XLA Ops:
  0.7 0.8 %copy.7.regs = f32[32,24]{1,0:T(8,128)S(1)} copy(f32[32,24]{0,1:T(8,128)} %param.7) | data formatting | bytes 6144 | tf_op args[1]
  1.4 0.0 copy-start.1
  1.4 0.0 copy-start.2
  1.4 1.1 %copy.8.vectors = bf16[704,64]{1,0:T(8,128)(2,1)S(1)} copy(bf16[704,64]{0,1:T(8,128)(2,1)} %param.11) | data formatting | bytes 180224 | tf_op args[5]
  2.5 0.0 copy-done.1
  2.5 0.0 copy-done.2
  2.5 0.0 copy-start
  2.5 1.0 %copy-done = bf16[32,5632]{1,0:T(8,128)(2,1)S(1)} copy-done((bf16[32,5632]{1,0:T(8,128)(2,1)S(1)}, bf16[32,5632]{1,0:T(8,128)(2,1)}, u32[]{:S(2)}) %copy-start) | copy-done | bytes 360472
  3.5 43.5 %shard_map.64 = f32[176,64]{1,0:T(8,128)S(1)} custom-call(bf16[32,5632]{1,0:T(8,128)(2,1)S(1)} %copy-done, f32[32,24]{1,0:T(8,128)S(1)} %copy.7.regs, s32[1,256]{1,0:T(1,128)S(1)} %bitcast.1, s32[1]{0:T(128)S(6)} %copy.10.count, s32[8]{0:T(128)S(1)} %copy-done.2, bf16[704,64]{1,0:T(8,128)(2,1)S(1)} %copy.8.vectors), custom_call_target="tpu_custom_call" | custom-call | tf_op jit(solution)/shard_map/pallas_call | solution.py:323
  47.0 0.7 %copy.9 = f32[176,64]{0,1:T(8,128)} copy(f32[176,64]{1,0:T(8,128)S(1)} %shard_map.64) | data formatting | bytes 90112 | tf_op jit(solution)/shard_map/pallas_call | solution.py:323
Async XLA Ops:
  1.4 1.1 %copy-start.1 = (s32[256]{0:T(256)S(1)}, s32[256]{0:T(256)}, u32[]{:S(2)}) copy-start(s32[256]{0:T(256)} %param.8) | copy-start | bytes 3076
  1.4 1.1 %copy-start.2 = (s32[8]{0:T(128)S(1)}, s32[8]{0:T(128)}, u32[]{:S(2)}) copy-start(s32[8]{0:T(128)} %owner.1) | copy-start | bytes 100
  2.5 1.0 %copy-start = (bf16[32,5632]{1,0:T(8,128)(2,1)S(1)}, bf16[32,5632]{1,0:T(8,128)(2,1)}, u32[]{:S(2)}) copy-start(bf16[32,5632]{1,0:T(8,128)(2,1)} %series.1) | copy-start | bytes 1081348

commit v2 on v0

--- a/solution.py
+++ b/solution.py
@@ -1,17 +1,284 @@
+import functools
 import math
 
 import jax
 import jax.numpy as jnp
 from jax import lax
+from jax.experimental import pallas as pl
+from jax.experimental.pallas import tpu as pltpu
 from jax.sharding import PartitionSpec as P
 
 BLOCKS = 8
-
+MESH = pl.DeviceIdType.MESH
+HIGHEST = lax.Precision.HIGHEST
 
 fast_pole = 0.64
 slow_pole = 0.955
 corr_limit = 0.99
 norm_eps = 1e-06
+
+
+def dot32(a, b, ca, cb):
+    return lax.dot_general(
+        a, b, (((ca,), (cb,)), ((), ())), precision=HIGHEST, preferred_element_type=jnp.float32
+    )
+
+
+def dot16(a, b, ca, cb):
+    return lax.dot_general(
+        a, b, (((ca,), (cb,)), ((), ())), preferred_element_type=jnp.float32
+    )
+
+
+def band_matrix(span_row):
+    frames = span_row.shape[1]
+    across = jnp.broadcast_to(span_row.astype(jnp.float32), (frames, frames))
+    down = across.T
+    lag = lax.broadcasted_iota(jnp.int32, (frames, frames), 0) - lax.broadcasted_iota(
+        jnp.int32, (frames, frames), 1
+    )
+    steps = jnp.maximum(lag, 0).astype(jnp.float32)
+    fast = (1.0 - fast_pole) * jnp.exp(steps * math.log(fast_pole))
+    slow = (1.0 - slow_pole) * jnp.exp(steps * math.log(slow_pole))
+    return jnp.where((lag >= 0) & (across == down), fast - slow, 0.0)
+
+
+def spd_inverse(gram):
+    size = gram.shape[0]
+    lane = lax.broadcasted_iota(jnp.int32, (size, size), 1)
+    sub = lax.broadcasted_iota(jnp.int32, (size, size), 0)
+
+    def sweep(k, m):
+        on_col, on_row = lane == k, sub == k
+        col = jnp.sum(jnp.where(on_col, m, 0.0), axis=1, keepdims=True)
+        row = jnp.sum(jnp.where(on_row, m, 0.0), axis=0, keepdims=True)
+        pivot = jnp.sum(jnp.where(on_col & on_row, m, 0.0), axis=(0, 1), keepdims=True)
+        inv = 1.0 / pivot
+        rest = m - col * (row * inv)
+        return jnp.where(
+            on_row,
+            jnp.where(on_col, inv, row * inv),
+            jnp.where(on_col, -col * inv, rest),
+        )
+
+    return lax.fori_loop(0, size, sweep, gram)
+
+
+def kernel(
+    series, regs, span, count, owner, vectors, out,
+    win, rows, nreg, vtb, a_hi, a_lo, unit, unit_rows, parts, other,
+    send, reg_r, win_r, vt_r, rows_r, fin_r, loc,
+):
+    grp, rep = lax.axis_index("grp"), lax.axis_index("rep")
+    z, x = grp // 2, grp % 2
+    y, c = rep // 2, rep % 2
+    groups = lax.axis_size("grp")
+    reps = lax.axis_size("rep")
+    nz = groups // 2
+    frames_loc, gray = series.shape
+    slab = gray // groups
+    part = 2 * slab
+    wide = rows.shape[1]
+    quarter = out.shape[1]
+    pair = y + c * (nz - 1 - 2 * y)
+    home = pair == z
+    away = pair != z
+
+    near = z + 1 - 2 * (z % 2)
+    far = [nz - 1 - z, lax.rem(z + nz // 2, nz)]
+    lines = [near] + far
+    x_peer = (z * 2 + 1 - x, rep)
+    diagonal = (near * 2 + 1 - x, rep)
+    direct = [(zz * 2 + x, rep) for zz in lines] + [x_peer, diagonal]
+    mates = [lax.rem(rep + d, reps) for d in range(1, reps)]
+
+    barrier = pltpu.get_barrier_semaphore()
+    everyone = direct + [(grp, k) for k in mates]
+    for peer in everyone:
+        pl.semaphore_signal(barrier, inc=1, device_id=peer, device_id_type=MESH)
+
+    sent = []
+
+    def push(src, dst, recv, peer, cond=None):
+        copy = pltpu.make_async_remote_copy(
+            src_ref=src, dst_ref=dst, send_sem=send.at[len(sent)], recv_sem=recv,
+            device_id=peer, device_id_type=MESH,
+        )
+        if cond is None:
+            copy.start()
+        else:
+            pl.when(cond)(copy.start)
+        sent.append((copy, cond))
+
+    def arrive(dst, recv):
+        pltpu.make_async_copy(dst, dst, recv).wait()
+
+    def rows_of(s):
+        return pl.ds(pl.multiple_of(s * frames_loc, frames_loc), frames_loc)
+
+    part_cols = pl.ds(pl.multiple_of(pair * part, 128), part)
+    slab_at = pl.multiple_of(grp * slab - (slab % 128) * x, 128)
+    slab_in_part = pl.ds(pl.multiple_of(x * (slab - slab % 128), 128), wide)
+
+    local_win = pltpu.make_async_copy(
+        series.at[:, part_cols], win.at[rows_of(grp), :], loc.at[0]
+    )
+    local_rows = pltpu.make_async_copy(
+        series.at[:, pl.ds(slab_at, wide)], rows.at[rows_of(grp), :], loc.at[1]
+    )
+    local_win.start()
+    local_rows.start()
+    nreg[grp] = regs[...]
+    nvec = vectors.shape[0]
+
+    @pl.when(home)
+    def _():
+        vtb[x] = vectors[...]
+
+    pl.semaphore_wait(barrier, len(everyone))
+
+    for peer in direct:
+        push(regs, nreg.at[grp], reg_r.at[grp], peer)
+    for peer in direct:
+        push(series.at[:, part_cols], win.at[rows_of(grp), :], win_r.at[grp], peer)
+    for peer in direct:
+        push(vectors, vtb.at[x], vt_r.at[x], peer, home)
+
+    filt = band_matrix(span[...])
+
+    for zz in far:
+        s = zz * 2 + x
+        arrive(nreg.at[s], reg_r.at[s])
+        push(nreg.at[s], nreg.at[s], reg_r.at[s], x_peer)
+    for s in [near * 2 + x] + [zz * 2 + 1 - x for zz in [z, near] + far]:
+        arrive(nreg.at[s], reg_r.at[s])
+
+    kmax = regs.shape[0]
+    active = (lax.broadcasted_iota(jnp.int32, (kmax, 1), 0) < count[0]).astype(jnp.float32)
+    frames_in = jnp.concatenate([nreg[s] for s in range(groups)], axis=1)
+    masked = dot32(frames_in, filt, 1, 1) * active
+    diag = (
+        lax.broadcasted_iota(jnp.int32, (kmax, kmax), 0)
+        == lax.broadcasted_iota(jnp.int32, (kmax, kmax), 1)
+    )
+    gram = dot32(masked, masked, 1, 1) + jnp.where(diag, 1.0 - active, 0.0)
+    inverse = spd_inverse(gram)
+
+    keeps = []
+
+    def landed(s, forward):
+        here = win.at[rows_of(s), :]
+        arrive(here, win_r.at[s])
+        if forward:
+            push(here, here, win_r.at[s], x_peer)
+        src = win.at[rows_of(s), slab_in_part]
+        dst = rows.at[rows_of(s), :]
+        for k in mates:
+            push(src, dst, rows_r.at[s], (grp, k), home)
+        keep = pltpu.make_async_copy(src, dst, loc.at[2 + len(keeps)])
+        pl.when(home)(keep.start)
+        keeps.append((keep, dst, rows_r.at[s]))
+
+    for zz in far:
+        landed(zz * 2 + x, True)
+    landed(near * 2 + x, False)
+    landed(z * 2 + 1 - x, False)
+    landed(near * 2 + 1 - x, False)
+
+    fitted = dot32(inverse, dot32(masked, filt, 1, 0), 1, 0)
+    clean = filt - dot32(masked, fitted, 0, 0)
+    clean = clean - jnp.mean(clean, axis=0, keepdims=True)
+    hi = clean.astype(jnp.bfloat16)
+    a_hi[...] = hi
+    a_lo[...] = (clean - hi.astype(jnp.float32)).astype(jnp.bfloat16)
+
+    pl.when(away)(lambda: arrive(vtb.at[x], vt_r.at[x]))
+    push(vtb.at[x], vtb.at[x], vt_r.at[x], x_peer, (pair != z) & (pair != near))
+
+    for zz in far:
+        landed(zz * 2 + 1 - x, False)
+    local_win.wait()
+    local_rows.wait()
+
+    def normal(block):
+        centered = dot16(a_hi[...], block, 1, 0) + dot16(a_lo[...], block, 1, 0)
+        power = jnp.mean(centered * centered, axis=0, keepdims=True) + norm_eps
+        return centered * (lax.rsqrt(power) * (1.0 / math.sqrt(centered.shape[0])))
+
+    for start in range(0, part, 256):
+        cols = slice(start, min(start + 256, part))
+        unit[:, cols] = normal(win[:, cols]).astype(jnp.bfloat16)
+
+    arrive(vtb.at[1 - x], vt_r.at[1 - x])
+    right = jnp.concatenate([vtb[t] for t in range(2)], axis=1)
+    place = lax.broadcasted_iota(jnp.int32, (1, part), 1)
+    which = 2 * pair + (place >= slab).astype(jnp.int32)
+    times = jnp.zeros((1, part), jnp.float32)
+    for b in range(BLOCKS):
+        times = times + jnp.where(which == owner[b], 0.5, 0.0)
+
+    for keep, dst, recv in keeps:
+        pl.when(away)(functools.partial(arrive, dst, recv))
+        pl.when(home)(keep.wait)
+    for start in range(0, wide, 256):
+        cols = slice(start, start + 256)
+        unit_rows[cols, :] = normal(rows[:, cols]).T.astype(jnp.bfloat16)
+
+    for k in mates + [rep]:
+        first = pl.multiple_of((slab % 128) * x + quarter * k, 16)
+        left = unit_rows[pl.ds(first, quarter), :]
+        corr = jnp.clip(dot16(left, unit[...], 1, 0), -corr_limit, corr_limit)
+        fisher = ((jnp.log(1.0 + corr) - jnp.log(1.0 - corr)) * times).astype(jnp.bfloat16)
+        parts[k] = dot16(right, fisher, 1, 1)
+        if k is not rep:
+            push(parts.at[k], other.at[rep], fin_r.at[rep], (grp, k))
+    total = parts[rep]
+    for k in mates:
+        arrive(other.at[k], fin_r.at[k])
+        total = total + other[k]
+    out[...] = total
+    for copy, cond in sent:
+        if cond is None:
+            copy.wait_send()
+        else:
+            pl.when(cond)(copy.wait_send)
+
+
+def one_kernel(series, regressors, span_ids, nuisance_count, owner_order, vectors):
+    groups, reps = lax.axis_size("grp"), lax.axis_size("rep")
+    frames_loc, gray = series.shape
+    frames = frames_loc * groups
+    slab = gray // groups
+    quarter = slab // reps
+    wide = -(-slab // 128) * 128
+    nvec = vectors.shape[1]
+    vm = pl.BlockSpec(memory_space=pltpu.VMEM)
+    sm = pl.BlockSpec(memory_space=pltpu.SMEM)
+    dma = pltpu.SemaphoreType.DMA
+    return pl.pallas_call(
+        kernel,
+        out_shape=jax.ShapeDtypeStruct((nvec, quarter), jnp.float32),
+        in_specs=[pl.BlockSpec(memory_space=pl.ANY), vm, vm, sm, sm, vm],
+        out_specs=vm,
+        scratch_shapes=[
+            pltpu.VMEM((frames, 2 * slab), jnp.bfloat16),
+            pltpu.VMEM((frames, wide), jnp.bfloat16),
+            pltpu.VMEM((groups, regressors.shape[1], frames_loc), jnp.float32),
+            pltpu.VMEM((2, nvec, slab), jnp.bfloat16),
+            pltpu.VMEM((frames, frames), jnp.bfloat16),
+            pltpu.VMEM((frames, frames), jnp.bfloat16),
+            pltpu.VMEM((frames, 2 * slab), jnp.bfloat16),
+            pltpu.VMEM((wide, frames), jnp.bfloat16),
+            pltpu.VMEM((reps, nvec, quarter), jnp.float32),
+            pltpu.VMEM((reps, nvec, quarter), jnp.float32),
+            dma((64,)),
+            dma((groups,)), dma((groups,)), dma((2,)),
+            dma((groups,)), dma((reps,)), dma((16,)),
+        ],
+        compiler_params=pltpu.CompilerParams(
+            collective_id=0, has_side_effects=True, vmem_limit_bytes=60 * 1024 * 1024
+        ),
+    )(series, regressors.T, span_ids[None, :], nuisance_count, owner_order, vectors.T).T
 
 
 def spread_2(value, axis, root):
@@ -96,7 +363,7 @@
     return running + jnp.dot(fisher, vec_slab, preferred_element_type=jnp.float32)
 
 
-def local(series, regressors, span_ids, nuisance_count, owner_order, vectors):
+def by_block(series, regressors, span_ids, nuisance_count, owner_order, vectors):
     grp_count = lax.axis_size("grp")
     rep_count = lax.axis_size("rep")
     rep_index = lax.axis_index("rep")
@@ -130,6 +397,7 @@
 
 
 def solution(mesh):
+    local = one_kernel if mesh.shape["grp"] == BLOCKS and mesh.shape["rep"] == 4 else by_block
     placed = (P("grp", None), P("grp", None), P(), P(), P(), P("grp", None))
     return jax.shard_map(
         local, mesh=mesh, in_specs=placed, out_specs=P(("grp", "rep"), None), check_vma=False

time: 232 us -> 36.7 us (0.16)
  waiting for transfers between devices: 95.1 us -> 0 us
  blocking collectives: 83.4 us -> 0 us
  Pallas kernels: 0 us -> 34 us
  between operations: 19.4 us -> 0.66 us
  other arithmetic: 8.9 us -> 0 us
  matrix products: 8.23 us -> 0 us
  starting transfers between devices: 7.29 us -> 0 us
  local copies, waits for them, and re-layouts: 8.67 us -> 1.47 us
    psum x1 -> x0, waiting for transfers between devices: 95.1 us -> none  [spread_2(): return lax.psum(jnp.where(mine, value, jnp.zeros_like(value)), axis)]
    all_gather x9 -> x0, blocking collectives: 83.4 us -> none  [the longest x8 52.3 us: local(): lax.all_gather(piece_in, 'rep', axis=1, tiled=True)]
    pallas_call x0 -> x1, Pallas kernels: none -> 34 us  [one_kernel(): pl.pallas_call(kernel, out_shape=jax.ShapeDtypeStruct((nvec, quarter), jn...]
    dot_general x19 -> x0, matrix products: 7.88 us -> none  [the longest x8 4.66 us: fold_tile(): jnp.dot(fisher, vec_slab, preferred_element_type=jnp.float32)]
    all_to_all x1 -> x0, starting transfers between devices: 7.25 us -> none  [local(): lax.all_to_all(quarter, 'grp', split_axis=1, concat_axis=0, tiled=True)]
    another operation x5 -> x0, other arithmetic: 5.37 us -> none  [the longest x3 2.87 us: nuisance_basis(): return (masked, jnp.linalg.cholesky(gram_matrix))]
    reshape x2 -> x0, local copies, waits for them, and re-layouts: 2.72 us -> none  [the longest x1 1.98 us: local(): quarter = series.reshape(frames_loc, grp_count, rep_count, own_cols)]
    select_n x3 -> x0, other arithmetic: 2.56 us -> none  [spread_2(): return lax.psum(jnp.where(mine, value, jnp.zeros_like(value)), axis)]
  transfers between devices with their start and end apart: 2 -> 0, of which waited for: 1 -> 0; matrix products, arithmetic and copies ran while one was open for 4% -> 0% of each run, Pallas kernels for 0% -> 0%
where the time goes in v2:
time: 36.7 us; the launch traced here: 36.1 us
  Pallas kernels  34 us (93%)
  local copies, waits for them, and re-layouts  1.47 us (4%)
  between operations  0.66 us (2%)
    pallas_call x1, Pallas kernels, one_kernel(): pl.pallas_call(kernel, out_shape=jax.ShapeDtypeStruct((nvec, quarter), jn...  34 us
    unnamed x1, local copies, waits for them, and re-layouts  1.47 us

profile of v2, /device:TPU:0, one launch (start us, length us, event | category | flops | bytes accessed | tf_op | source)
XLA Modules:
  0.0 36.1 jit_solution(9756615844392223166)
XLA Ops:
  0.7 34.0 %shard_map.64 = f32[64,176]{1,0:T(8,128)} custom-call(bf16[32,5632]{1,0:T(8,128)(2,1)} %series.1, f32[24,32]{1,0:T(8,128)} %bitcast.6, s32[1,256]{1,0:T(1,128)} %bitcast.7, s32[1]{0:T(128)S(6)} %copy.8.count, s32[8]{0:T(128)} %owner.1, bf16[64,704]{1,0:T(8,128)(2,1)} %bitcast.5), custom_call_target="tpu_custom_call" | custom-call | tf_op jit(solution)/shard_map/pallas_call | solution.py:258
  34.6 1.5 %copy.9 = f32[176,64]{0,1:T(8,128)} copy(f32[176,64]{0,1:T(8,128)} %bitcast.4) | data formatting | bytes 90112

commit v3 on v2

--- a/solution.py
+++ b/solution.py
@@ -86,14 +86,14 @@
 
     near = z + 1 - 2 * (z % 2)
     far = [nz - 1 - z, lax.rem(z + nz // 2, nz)]
-    lines = [near] + far
     x_peer = (z * 2 + 1 - x, rep)
     diagonal = (near * 2 + 1 - x, rep)
-    direct = [(zz * 2 + x, rep) for zz in lines] + [x_peer, diagonal]
+    direct = [(zz * 2 + x, rep) for zz in [near] + far] + [x_peer, diagonal]
     mates = [lax.rem(rep + d, reps) for d in range(1, reps)]
 
     barrier = pltpu.get_barrier_semaphore()
-    everyone = direct + [(grp, k) for k in mates]
+    across = [(zz * 2 + 1 - x, rep) for zz in far]
+    everyone = direct + across + [(grp, k) for k in mates]
     for peer in everyone:
         pl.semaphore_signal(barrier, inc=1, device_id=peer, device_id_type=MESH)
 
@@ -137,19 +137,15 @@
 
     pl.semaphore_wait(barrier, len(everyone))
 
-    for peer in direct:
+    for peer in direct + across:
         push(regs, nreg.at[grp], reg_r.at[grp], peer)
     for peer in direct:
         push(series.at[:, part_cols], win.at[rows_of(grp), :], win_r.at[grp], peer)
-    for peer in direct:
-        push(vectors, vtb.at[x], vt_r.at[x], peer, home)
-
     filt = band_matrix(span[...])
 
     for zz in far:
         s = zz * 2 + x
         arrive(nreg.at[s], reg_r.at[s])
-        push(nreg.at[s], nreg.at[s], reg_r.at[s], x_peer)
     for s in [near * 2 + x] + [zz * 2 + 1 - x for zz in [z, near] + far]:
         arrive(nreg.at[s], reg_r.at[s])
 
@@ -181,6 +177,9 @@
 
     for zz in far:
         landed(zz * 2 + x, True)
+    for peer in direct[:-1]:
+        push(vectors, vtb.at[x], vt_r.at[x], peer, home)
+
     landed(near * 2 + x, False)
     landed(z * 2 + 1 - x, False)
     landed(near * 2 + 1 - x, False)
@@ -193,7 +192,7 @@
     a_lo[...] = (clean - hi.astype(jnp.float32)).astype(jnp.bfloat16)
 
     pl.when(away)(lambda: arrive(vtb.at[x], vt_r.at[x]))
-    push(vtb.at[x], vtb.at[x], vt_r.at[x], x_peer, (pair != z) & (pair != near))
+    push(vtb.at[x], vtb.at[x], vt_r.at[x], x_peer, away)
 
     for zz in far:
         landed(zz * 2 + 1 - x, False)

time: 36.7 us -> 35.8 us (0.975)
  Pallas kernels: 34 us -> 33.4 us
    pallas_call x1, Pallas kernels: 34 us -> 33.4 us  [one_kernel(): pl.pallas_call(kernel, out_shape=jax.ShapeDtypeStruct((nvec, quarter), jn...]
where the time goes in v3:
time: 35.8 us; the launch traced here: 35.6 us
  Pallas kernels  33.4 us (93%)
  local copies, waits for them, and re-layouts  1.47 us (4%)
  between operations  0.66 us (2%)
    pallas_call x1, Pallas kernels, one_kernel(): pl.pallas_call(kernel, out_shape=jax.ShapeDtypeStruct((nvec, quarter), jn...  33.4 us
    unnamed x1, local copies, waits for them, and re-layouts  1.47 us

profile of v3, /device:TPU:0, one launch (start us, length us, event | category | flops | bytes accessed | tf_op | source)
XLA Modules:
  0.0 35.6 jit_solution(11650581860012917174)
XLA Ops:
  0.7 33.4 %shard_map.64 = f32[64,176]{1,0:T(8,128)} custom-call(bf16[32,5632]{1,0:T(8,128)(2,1)} %series.1, f32[24,32]{1,0:T(8,128)} %bitcast.6, s32[1,256]{1,0:T(1,128)} %bitcast.7, s32[1]{0:T(128)S(6)} %copy.8.count, s32[8]{0:T(128)} %owner.1, bf16[64,704]{1,0:T(8,128)(2,1)} %bitcast.5), custom_call_target="tpu_custom_call" | custom-call | tf_op jit(solution)/shard_map/pallas_call | solution.py:257
  34.1 1.5 %copy.9 = f32[176,64]{0,1:T(8,128)} copy(f32[176,64]{0,1:T(8,128)} %bitcast.4) | data formatting | bytes 90112
